TPU v7x, 32 devices: a whole 2x2x4 slice. The times are simulated.
32 devices in a mesh: slide: 2 (over y), seq: 16 (over z, x, core), head: 1.
Axes of the slice: x: 2, y: 2, z: 4, core: 2. Of those that a mesh axis runs over, the one named last changes fastest.
Arguments:
- queries: bfloat16 [16384, 768], P(('slide', 'seq'), 'head'), parts along dimension 0, may hold values from -14 to 14
- key_states: bfloat16 [16384, 768], P(('slide', 'seq'), 'head'), parts along dimension 0, may hold values from -4 to 4
- value_states: bfloat16 [16384, 768], P(('slide', 'seq'), 'head'), parts along dimension 0, may hold values from -6 to 6
- offsets_mid: int32 [16], replicated, may hold values from 0 to 3
- offsets_top: int32 [16], replicated, may hold values from 0 to 3
- out_weight: bfloat16 [768, 768], P('head'), may hold values from -0.21875 to 0.21875
Outputs:
- projected: bfloat16 [16384, 768], P(('slide', 'seq', 'head')), parts along dimension 0
There are 2 independent parts, one for each index of `slide`. A program takes and returns all parts, laid end to end along the dimension named above; an argument that names none is the same for every part. Nothing has to cross between parts.
All inputs are finite; a program needn't handle non-finite values.
Results may differ from a plain program's by a relative error of at most 0.0052.
Values may be sent and summed in bfloat16 or wider, within the bound.
No kernel may reach another device: no remote copies, remote signals or barrier semaphores. Data moves between devices by JAX's collectives and lax.ppermute only.
A program may use at most 64 MiB of HBM per device.

v0:
```python
import jax
import jax.numpy as jnp
from jax import lax
from jax.sharding import PartitionSpec as P

SEG = 2048


def partner_2(block, axis, apart):
    count = lax.axis_size(axis)
    route = []
    for low in range(count):
        high = low | 1 << apart
        if high != low and high < count:
            route += [(low, high), (high, low)]
    return lax.ppermute(block, axis, route)


def attend_head(triple_in):
    query_rows, key_rows, value_rows = triple_in
    score_scale = query_rows.shape[-1] ** (-0.5)
    scores = jnp.dot(query_rows, key_rows.T, preferred_element_type=jnp.float32) * score_scale
    row_max = jnp.max(scores, axis=1)
    shifted = jnp.exp(scores - row_max[:, None])
    row_total = jnp.sum(shifted, axis=1)
    weights = shifted.astype(jnp.bfloat16)
    numerator = jnp.dot(weights, value_rows, preferred_element_type=jnp.float32)
    return (numerator, row_total, row_max)


def attend_local(query_rows, pair_rows):
    return lax.map(
        attend_head,
        (
            query_rows.transpose(1, 0, 2),
            pair_rows[:, 0].transpose(1, 0, 2),
            pair_rows[:, 1].transpose(1, 0, 2),
        ),
    )


def pick_rows(states, offsets, rate):
    row_count, inner_count, heads_here, head_width = states.shape
    picker = (jnp.arange(rate)[:, None] == offsets[None, :]).astype(jnp.bfloat16)
    folded = states.reshape(row_count // rate, rate, inner_count, heads_here, head_width)
    return jnp.einsum("archd,rh->achd", folded, picker, preferred_element_type=jnp.float32).astype(
        jnp.bfloat16
    )


def spread_back(numerator, row_total, row_max, offsets, rate):
    heads_here, picked_count, head_width = numerator.shape
    chosen = jnp.arange(rate)[:, None] == offsets[None, :]
    full_num = jnp.where(chosen[None, :, :, None], numerator.transpose(1, 0, 2)[:, None], 0.0)
    full_total = jnp.where(chosen[None], row_total.T[:, None], 0.0)
    full_max = jnp.where(chosen[None], row_max.T[:, None], -1e30)
    return (
        full_num.reshape(picked_count * rate, heads_here, head_width),
        full_total.reshape(picked_count * rate, heads_here),
        full_max.reshape(picked_count * rate, heads_here),
    )


def doubling(buffer, steps_count, section_index):
    position = lax.axis_index("seq")
    for bit_index in range(steps_count):
        if section_index == 0:
            partner = partner_2(buffer, "seq", bit_index)
        else:
            partner = partner_2(buffer, "seq", bit_index)
        is_lower = position >> bit_index & 1 == 0
        buffer = jnp.where(
            is_lower, jnp.concatenate([buffer, partner], 0), jnp.concatenate([partner, buffer], 0)
        )
    return buffer


def shards(queries, key_states, value_states, offsets_mid, offsets_top, out_weight):
    tok_rows = queries.shape[0]
    heads_local = offsets_mid.shape[0] // lax.axis_size("head")
    head_size = queries.shape[1] // heads_local
    seq_devices = lax.axis_size("seq")
    seq_total = tok_rows * seq_devices
    width_mid = min(16 * SEG, seq_total)
    rate_mid = width_mid // SEG
    rate_top = seq_total // SEG
    start_head = lax.axis_index("head") * heads_local
    mid_local = lax.dynamic_slice(offsets_mid, (start_head,), (heads_local,))
    top_local = lax.dynamic_slice(offsets_top, (start_head,), (heads_local,))
    query_heads = queries.reshape(tok_rows, 1, heads_local, head_size)
    paired = jnp.stack([key_states, value_states], axis=1).reshape(
        tok_rows, 2, heads_local, head_size
    )
    near_bits = (SEG // tok_rows).bit_length() - 1
    near_rows = doubling(paired.reshape(tok_rows, -1), near_bits, 0).reshape(
        SEG, 2, heads_local, head_size
    )
    near_num, near_total, near_max = attend_local(query_heads[:, 0], near_rows)
    level_near = spread_back(
        near_num, near_total, near_max, jnp.zeros((heads_local,), jnp.int32), 1
    )
    mid_q = pick_rows(query_heads, mid_local, rate_mid)[:, 0]
    mid_kv = pick_rows(paired, mid_local, rate_mid)
    mid_group = width_mid // tok_rows
    mid_bits = mid_group.bit_length() - 1
    mid_rows = doubling(mid_kv.reshape(mid_kv.shape[0], -1), mid_bits, 1).reshape(
        SEG, 2, heads_local, head_size
    )
    mid_num, mid_total, mid_max = attend_local(mid_q, mid_rows)
    level_mid = spread_back(mid_num, mid_total, mid_max, mid_local, rate_mid)
    top_q = pick_rows(query_heads, top_local, rate_top)[:, 0]
    top_kv = pick_rows(paired, top_local, rate_top)
    top_rows = lax.all_gather(
        top_kv.reshape(top_kv.shape[0], -1), "seq", axis=0, tiled=True
    ).reshape(SEG, 2, heads_local, head_size)
    top_num, top_total, top_max = attend_local(top_q, top_rows)
    level_top = spread_back(top_num, top_total, top_max, top_local, rate_top)
    levels = [level_near, level_mid, level_top]
    overall = jnp.maximum(jnp.maximum(level_near[2], level_mid[2]), level_top[2])
    numerator = jnp.zeros((tok_rows, heads_local, head_size), jnp.float32)
    row_total = jnp.zeros((tok_rows, heads_local), jnp.float32)
    for level_num, level_total, level_max in levels:
        factor = jnp.exp(level_max - overall)
        numerator = numerator + factor[..., None] * level_num
        row_total = row_total + factor * level_total
    attention = (
        (numerator / row_total[..., None])
        .astype(jnp.bfloat16)
        .reshape(tok_rows, heads_local * head_size)
    )
    result = lax.psum_scatter(
        jnp.dot(attention, out_weight, preferred_element_type=jnp.float32),
        "head",
        scatter_dimension=0,
        tiled=True,
    )
    return result.astype(jnp.bfloat16)


def solution(mesh):
    in_specs = (
        P(("slide", "seq"), "head"),
        P(("slide", "seq"), "head"),
        P(("slide", "seq"), "head"),
        P(),
        P(),
        P("head", None),
    )
    out_specs = P(("slide", "seq", "head"), None)
    return jax.shard_map(shards, mesh=mesh, in_specs=in_specs, out_specs=out_specs, check_vma=False)
```

profile of v0, /device:TPU:0, one launch (start us, length us, event | category | flops | bytes accessed | tf_op | source)
XLA Modules:
  0.0 416.9 jit_solution(6318891818298595797)
XLA Ops:
  11.7 3.5 stack.28
  15.2 3.5 stack.27
  18.7 4.0 copy.96
  22.7 2.9 copy.95
  32.3 2.7 collective-permute-start.3
  35.0 5.1 %maximum_select_fusion.3 = bf16[1024,1536]{0,1:T(8,128)(2,1)} fusion(bf16[512,1536]{0,1:T(8,128)(2,1)} %collective-permute-done, bf16[512,1536]{0,1:T(8,128)(2,1)} %bitcast.28, pred[]{:T(512)S(6)} %eq.37), kind=kLoop, calls=%fused_computation.60 | loop fusion | flops 14155776 | bytes 6291457 | tf_op jit(solution)/shard_map/jit(_where)/select_n | solution.py:72
  40.1 13.3 %collective-permute-done.3 = bf16[256,1536]{0,1:T(8,128)(2,1)S(1)} collective-permute-done((bf16[256,1536]{0,1:T(8,128)(2,1)S(1)}, bf16[256,1536]{0,1:T(8,128)(2,1)S(1)}, u32[]{:S(2)}, u32[]{:S(2)}) %collective-permute-start.3) | collective-permute-done | bytes 786464 | tf_op jit(solution)/shard_map/ppermute | solution.py:16
  54.9 2.1 collective-permute-start.4
  57.1 2.7 fusion.51
  61.9 3.7 reshape.246
  67.7 2.2 fusion.46
  72.5 2.0 copy.156
  76.5 2.5 maximum_select_fusion.2
  79.0 24.6 %collective-permute-done.4 = bf16[512,1536]{0,1:T(8,128)(2,1)} collective-permute-done((bf16[512,1536]{0,1:T(8,128)(2,1)}, bf16[512,1536]{0,1:T(8,128)(2,1)}, u32[]{:S(2)}, u32[]{:S(2)}) %collective-permute-start.4) | collective-permute-done | bytes 1572896 | tf_op jit(solution)/shard_map/ppermute | solution.py:16
  103.6 5.3 %maximum_select_fusion.5 = bf16[1024,1536]{0,1:T(8,128)(2,1)} fusion(bf16[512,1536]{0,1:T(8,128)(2,1)} %collective-permute-done.4, bf16[512,1536]{0,1:T(8,128)(2,1)} %maximum_select_fusion.7, pred[]{:T(512)S(6)} %eq.42), kind=kLoop, calls=%fused_computation.62 | loop fusion | flops 14155776 | bytes 6291457 | tf_op jit(solution)/shard_map/jit(_where)/select_n | solution.py:72
  108.9 2.6 collective-permute-start.5
  111.5 4.0 maximum_select_fusion.4
  115.5 26.1 %collective-permute-done.1 = bf16[1024,1536]{0,1:T(8,128)(2,1)} collective-permute-done((bf16[1024,1536]{0,1:T(8,128)(2,1)}, bf16[1024,1536]{0,1:T(8,128)(2,1)}, u32[]{:S(2)}, u32[]{:S(2)}) %collective-permute-start.1) | collective-permute-done | bytes 3145760 | tf_op jit(solution)/shard_map/ppermute | solution.py:16
  141.7 4.8 %maximum_select_fusion = bf16[2048,2,16,48]{0,3,2,1:T(8,128)(2,1)S(1)} fusion(bf16[1024,2,16,48]{0,3,2,1:T(8,128)(2,1)} %bitcast.30, bf16[1024,2,16,48]{0,3,2,1:T(8,128)(2,1)S(1)} %maximum_select_fusion.2, pred[]{:T(512)S(6)} %eq.36), kind=kLoop, calls=%fused_computation.47 | loop fusion | flops 28311552 | bytes 12582913 | tf_op jit(solution)/shard_map/jit(_where)/select_n | solution.py:72
  146.5 3.2 slice_bitcast_fusion.4
  149.7 113.8 %while.42 = (s32[]{:T(128)}, f32[16,512,48]{1,2,0:T(8,128)S(1)}, f32[16,512]{1,0:T(8,128)}, f32[16,512]{1,0:T(8,128)}, bf16[16,512,48]{1,2,0:T(8,128)(2,1)}, /*i...) while((s32[]{:T(128)}, f32[16,512,48]{1,2,0:T(8,128)S(1)}, ...), condition=%wide.region_3.4_spmd, body=%wide.region_0.3_spmd.sunk | while | flops 209714176 | bytes 13142125 | solution.py:32
  263.5 4.5 %collective-permute-done.5 = bf16[1024,1536]{0,1:T(8,128)(2,1)} collective-permute-done((bf16[1024,1536]{0,1:T(8,128)(2,1)}, bf16[1024,1536]{0,1:T(8,128)(2,1)}, u32[]{:S(2)}, u32[]{:S(2)}) %collective-permute-start.5) | collective-permute-done | bytes 3145760 | tf_op jit(solution)/shard_map/ppermute | solution.py:16
  268.1 6.8 %maximum_select_fusion.1 = bf16[2048,2,16,48]{0,3,2,1:T(8,128)(2,1)S(1)} fusion(bf16[1024,2,16,48]{0,3,2,1:T(8,128)(2,1)} %bitcast.45, bf16[1024,2,16,48]{0,3,2,1:T(8,128)(2,1)} %maximum_select_fusion.4, pred[]{:T(512)S(6)} %eq.41), kind=kLoop, calls=%fused_computation.48 | loop fusion | flops 28311552 | bytes 12582913 | tf_op jit(solution)/shard_map/jit(_where)/select_n | solution.py:72
  274.9 3.2 slice_bitcast_fusion.2
  278.2 47.9 %while.43 = (s32[]{:T(128)}, f32[16,128,48]{1,2,0:T(8,128)S(1)}, f32[16,128]{1,0:T(8,128)S(1)}, f32[16,128]{1,0:T(8,128)S(1)}, bf16[16,128,48]{2,1,0:T(8,128)(2,...) while((s32[]{:T(128)}, f32[16,128,48]{1,2,0:T(8,128)S(1)}, ...), condition=%wide.region_7.8_spmd, body=%wide.region_4.7_spmd.sunk | while | flops 51904256 | bytes 3602541 | solution.py:32
  327.1 2.4 broadcast_in_dim.202
  329.4 4.7 %broadcast_in_dim.203 = f32[512,768]{1,0:T(8,128)} reshape(f32[128,4,16,48]{3,2,1,0:T(8,128)} %broadcast_in_dim.202) | data formatting | bytes 3145728 | tf_op jit(solution)/shard_map/jit(_where)/broadcast_in_dim | solution.py:54
  336.1 6.6 %slice_bitcast_fusion = (bf16[16,2048,48]{1,2,0:T(8,128)(2,1)}, bf16[16,2048,48]{1,2,0:T(8,128)(2,1)}) fusion(bf16[2048,2,16,48]{0,3,2,1:T(8,128)(2,1)} %bitcast.238), kind=kLoop, calls=%fused_computation.53 | loop fusion | bytes 12582912 | tf_op jit(solution)/shard_map/transpose | solution.py:37
  342.7 47.9 %while.44 = (s32[]{:T(128)}, f32[16,128,48]{1,2,0:T(8,128)S(1)}, f32[16,128]{1,0:T(8,128)S(1)}, f32[16,128]{1,0:T(8,128)S(1)}, bf16[16,128,48]{2,1,0:T(8,128)(2,...) while((s32[]{:T(128)}, f32[16,128,48]{1,2,0:T(8,128)S(1)}, ...), condition=%wide.region_11.12_spmd, body=%wide.region_8.11_spmd.sunk | while | flops 51904256 | bytes 3602541 | solution.py:32
  394.4 3.5 broadcast_in_dim.207
  397.9 4.8 %broadcast_in_dim.208 = f32[512,768]{1,0:T(8,128)} reshape(f32[128,4,16,48]{3,2,1,0:T(8,128)} %broadcast_in_dim.207) | data formatting | bytes 3145728 | tf_op jit(solution)/shard_map/jit(_where)/broadcast_in_dim | solution.py:54
  402.7 3.0 copy.112
  (339 shorter events, 241.8 us)
Async XLA Ops:
  6.5 401.8 %copy-start = (bf16[768,768]{1,0:T(8,128)(2,1)S(1)}, bf16[768,768]{1,0:T(8,128)(2,1)}, u32[]{:S(2)}) copy-start(bf16[768,768]{1,0:T(8,128)(2,1)} %param.17) | copy-start | bytes 3538948
  6.5 5.1 %copy-start.7 = (bf16[512,768]{1,0:T(8,128)(2,1)S(1)}, bf16[512,768]{1,0:T(8,128)(2,1)}, u32[]{:S(2)}) copy-start(bf16[512,768]{1,0:T(8,128)(2,1)} %param.14) | copy-start | bytes 2359300
  6.5 329.5 %all-gather.2.cloned.1.call-start = ((), (), s32[]{:S(2)}) async-start(), calls=%async_computation | async-start | bytes 6684672 | tf_op jit(solution)/shard_map/all_gather | solution.py:113
  8.1 3.6 copy-start.1
  9.8 1.9 copy-start.3
  11.2 23.8 %collective-permute-start = (bf16[512,1536]{0,1:T(8,128)(2,1)}, bf16[512,1536]{0,1:T(8,128)(2,1)}, u32[]{:S(2)}, u32[]{:S(2)}) collective-permute-start(bf16[512,1536]{0,1:T(8,128)(2,1)} %bitcast.28), channel_id=1, source_target_pairs={{0,1},{1,0},{2,3},{3,2},{4,5},{5,4},{6,7},{7,6},{8,9},{9,8},{10,11... | collective-permute-start | bytes 4718600 | tf_op jit(solution)/shard_map/ppermute | solution.py:16
  18.7 6.9 %copy-start.19 = (s32[16]{0:T(128)S(1)}, s32[16]{0:T(128)}, u32[]{:S(2)}) copy-start(s32[16]{0:T(128)} %param.15) | copy-start | bytes 196
  18.7 6.9 %copy-start.20 = (s32[16]{0:T(128)S(1)}, s32[16]{0:T(128)}, u32[]{:S(2)}) copy-start(s32[16]{0:T(128)} %param.16) | copy-start | bytes 196
  27.2 2.3 copy-start.13
  28.5 0.9 copy-start.6
  29.5 1.8 collective-permute-start.2
  31.3 0.7 copy-start.14
  32.3 21.1 %collective-permute-start.3 = (bf16[256,1536]{0,1:T(8,128)(2,1)S(1)}, bf16[256,1536]{0,1:T(8,128)(2,1)S(1)}, u32[]{:S(2)}, u32[]{:S(2)}) collective-permute-start(bf16[256,1536]{0,1:T(8,128)(2,1)S(1)} %maximum_select_fusion.9), channel_id=1, source_target_pairs={{0,2},{2,0},{1,3},{3,1},{4,6},{6,4},{5,7},{7,5},{8,10},{10,8},{9,1... | collective-permute-start | bytes 2359304 | tf_op jit(solution)/shard_map/ppermute | solution.py:16
  40.1 101.5 %collective-permute-start.1 = (bf16[1024,1536]{0,1:T(8,128)(2,1)}, bf16[1024,1536]{0,1:T(8,128)(2,1)}, u32[]{:S(2)}, u32[]{:S(2)}) collective-permute-start(bf16[1024,1536]{0,1:T(8,128)(2,1)} %maximum_select_fusion.3), channel_id=1, source_target_pairs={{0,2},{2,0},{1,3},{3,1},{4,6},{6,4},{5,7},{7,5},{8,10},{10,8},{9,1... | collective-permute-start | bytes 9437192 | tf_op jit(solution)/shard_map/ppermute | solution.py:16
  53.4 6.4 %copy-start.9 = (bf16[256,1536]{0,1:T(8,128)(2,1)}, bf16[256,1536]{0,1:T(8,128)(2,1)S(1)}, u32[]{:S(2)}) copy-start(bf16[256,1536]{0,1:T(8,128)(2,1)S(1)} %collective-permute-done.3) | copy-start | bytes 2359300
  54.9 5.8 %copy-start.8 = (bf16[512,768]{1,0:T(8,128)(2,1)S(1)}, bf16[512,768]{1,0:T(8,128)(2,1)}, u32[]{:S(2)}) copy-start(bf16[512,768]{1,0:T(8,128)(2,1)} %param.12) | copy-start | bytes 2359300
  54.9 48.7 %collective-permute-start.4 = (bf16[512,1536]{0,1:T(8,128)(2,1)}, bf16[512,1536]{0,1:T(8,128)(2,1)}, u32[]{:S(2)}, u32[]{:S(2)}) collective-permute-start(bf16[512,1536]{0,1:T(8,128)(2,1)} %maximum_select_fusion.7), channel_id=1, source_target_pairs={{0,4},{4,0},{1,5},{5,1},{2,6},{6,2},{3,7},{7,3},{8,12},{12,8},{9,1... | collective-permute-start | bytes 4718600 | tf_op jit(solution)/shard_map/ppermute | solution.py:16
  69.9 6.2 %copy-start.10 = (bf16[256,1536]{0,1:T(8,128)(2,1)S(1)}, bf16[256,1536]{0,1:T(8,128)(2,1)}, u32[]{:S(2)}) copy-start(bf16[256,1536]{0,1:T(8,128)(2,1)} %copy-done.9) | copy-start | bytes 2359300
  70.8 5.7 %copy-start.2 = (bf16[512,768]{0,1:T(8,128)(2,1)S(1)}, bf16[512,768]{0,1:T(8,128)(2,1)}, u32[]{:S(2)}) copy-start(bf16[512,768]{0,1:T(8,128)(2,1)} %copy-done.1) | copy-start | bytes 2359300
  70.8 5.7 %copy-start.4 = (bf16[512,768]{0,1:T(8,128)(2,1)S(1)}, bf16[512,768]{0,1:T(8,128)(2,1)}, u32[]{:S(2)}) copy-start(bf16[512,768]{0,1:T(8,128)(2,1)} %copy-done.3) | copy-start | bytes 2359300
  108.9 159.1 %collective-permute-start.5 = (bf16[1024,1536]{0,1:T(8,128)(2,1)}, bf16[1024,1536]{0,1:T(8,128)(2,1)}, u32[]{:S(2)}, u32[]{:S(2)}) collective-permute-start(bf16[1024,1536]{0,1:T(8,128)(2,1)} %maximum_select_fusion.5), channel_id=1, source_target_pairs={{0,8},{8,0},{1,9},{9,1},{2,10},{10,2},{3,11},{11,3},{4,12},{12,4},... | collective-permute-start | bytes 9437192 | tf_op jit(solution)/shard_map/ppermute | solution.py:16
  146.5 3.2 copy-start.11
  263.5 11.4 %copy-start.12 = (f32[16,512,48]{1,2,0:T(8,128)}, f32[16,512,48]{1,2,0:T(8,128)S(1)}, u32[]{:S(2)}) copy-start(f32[16,512,48]{1,2,0:T(8,128)S(1)} %get-tuple-element.125) | copy-start | bytes 4718596
  390.6 0.6 copy-start.16
  397.9 7.8 %copy-start.15 = (f32[512,16]{0,1:T(8,128)S(1)}, f32[512,16]{0,1:T(8,128)}, u32[]{:S(2)}) copy-start(f32[512,16]{0,1:T(8,128)} %copy.118) | copy-start | bytes 98308
  397.9 7.8 %copy-start.17 = (f32[16,512]{1,0:T(8,128)S(1)}, f32[16,512]{1,0:T(8,128)}, u32[]{:S(2)}) copy-start(f32[16,512]{1,0:T(8,128)} %get-tuple-element.128) | copy-start | bytes 98308
  397.9 7.8 %copy-start.18 = (f32[16,512]{1,0:T(8,128)S(1)}, f32[16,512]{1,0:T(8,128)}, u32[]{:S(2)}) copy-start(f32[16,512]{1,0:T(8,128)} %get-tuple-element.122) | copy-start | bytes 98308
  405.8 1.9 copy-start.5
Sparse Core Ops, SparseCore 0:
  60.8 154.4 all-gather.1
where the time goes:
time: 421 us; the launch traced here: 417 us
  matrix products  147 us (35%)
  local copies, waits for them, and re-layouts  115 us (27%)
  waiting for transfers between devices  70.3 us (17%)
  other arithmetic  62.4 us (15%)
  between operations  13.8 us (3%)
  starting transfers between devices  7.97 us (2%)
    dot_general x48, matrix products, attend_head(): numerator = jnp.dot(weights, value_rows, preferred_element_type=jnp.float32)  71.2 us
    ppermute x6, waiting for transfers between devices, partner_2(): return lax.ppermute(block, axis, route)  70.2 us
    dot_general x48, matrix products, attend_head(): jnp.dot(query_rows, key_rows.T, preferred_element_type=jnp.float32)  69.9 us
    dynamic_update_slice x96, local copies, waits for them, and re-layouts, attend_local(): lax.map(attend_head, (query_rows.transpose(1, 0, 2), pair_rows[:, 0].tran...  45 us
    select_n x10, other arithmetic, doubling(): jnp.where(is_lower, jnp.concatenate([buffer, partner], 0), jnp.concatenat...  32.3 us
    reduce_sum x48, other arithmetic, attend_head(): row_total = jnp.sum(shifted, axis=1)  22.5 us
    broadcast_in_dim x6, local copies, waits for them, and re-layouts, spread_back(): jnp.where(chosen[None, :, :, None], numerator.transpose(1, 0, 2)[:, None]...  20.3 us
    another operation x4, local copies, waits for them, and re-layouts, shards(): jnp.stack([key_states, value_states], axis=1)  13.9 us
  transfers between devices with their start and end apart: 7, of which 5 were waited for; matrix products, arithmetic and copies ran while one was open for 59% of the time, Pallas kernels for 0%

commit v1 on v0

--- a/solution.py
+++ b/solution.py
@@ -1,9 +1,18 @@
+import functools
+
 import jax
 import jax.numpy as jnp
 from jax import lax
+from jax.experimental import pallas as pl
+from jax.experimental.pallas import tpu as pltpu
 from jax.sharding import PartitionSpec as P
 
 SEG = 2048
+LOG2E = 1.4426950408889634
+VMEM_LIMIT = 40 * 1024 * 1024
+VMEM_MOST = 60 * 1024 * 1024
+BF16 = jnp.bfloat16
+F32 = jnp.float32
 
 
 def partner_2(block, axis, apart):
@@ -61,13 +70,10 @@
     )
 
 
-def doubling(buffer, steps_count, section_index):
+def doubling(buffer, steps_count):
     position = lax.axis_index("seq")
     for bit_index in range(steps_count):
-        if section_index == 0:
-            partner = partner_2(buffer, "seq", bit_index)
-        else:
-            partner = partner_2(buffer, "seq", bit_index)
+        partner = partner_2(buffer, "seq", bit_index)
         is_lower = position >> bit_index & 1 == 0
         buffer = jnp.where(
             is_lower, jnp.concatenate([buffer, partner], 0), jnp.concatenate([partner, buffer], 0)
@@ -75,7 +81,7 @@
     return buffer
 
 
-def shards(queries, key_states, value_states, offsets_mid, offsets_top, out_weight):
+def shards_general(queries, key_states, value_states, offsets_mid, offsets_top, out_weight):
     tok_rows = queries.shape[0]
     heads_local = offsets_mid.shape[0] // lax.axis_size("head")
     head_size = queries.shape[1] // heads_local
@@ -92,7 +98,7 @@
         tok_rows, 2, heads_local, head_size
     )
     near_bits = (SEG // tok_rows).bit_length() - 1
-    near_rows = doubling(paired.reshape(tok_rows, -1), near_bits, 0).reshape(
+    near_rows = doubling(paired.reshape(tok_rows, -1), near_bits).reshape(
         SEG, 2, heads_local, head_size
     )
     near_num, near_total, near_max = attend_local(query_heads[:, 0], near_rows)
@@ -103,7 +109,7 @@
     mid_kv = pick_rows(paired, mid_local, rate_mid)
     mid_group = width_mid // tok_rows
     mid_bits = mid_group.bit_length() - 1
-    mid_rows = doubling(mid_kv.reshape(mid_kv.shape[0], -1), mid_bits, 1).reshape(
+    mid_rows = doubling(mid_kv.reshape(mid_kv.shape[0], -1), mid_bits).reshape(
         SEG, 2, heads_local, head_size
     )
     mid_num, mid_total, mid_max = attend_local(mid_q, mid_rows)
@@ -137,6 +143,426 @@
     return result.astype(jnp.bfloat16)
 
 
+RATE = 4
+GROUP = 4
+HG = 4
+DH = 48
+BLK = 128
+HALF = 2 * BLK
+TOK = 512
+DX = 64
+
+
+def dot(a, b):
+    return jnp.dot(a, b, preferred_element_type=F32)
+
+
+def dot_nt(a, b):
+    return lax.dot_general(a, b, (((1,), (1,)), ((), ())), preferred_element_type=F32)
+
+
+def class_of_slots(off_mid, off_top):
+    first = off_mid
+    second = jnp.where(off_top == off_mid, lax.rem(off_mid + 1, RATE), off_top)
+    free0 = (first != 0) & (second != 0)
+    free1 = (first != 1) & (second != 1)
+    third = jnp.where(free0, 0, jnp.where(free1, 1, 2))
+    return first, second, third, 6 - first - second - third
+
+
+def head_of(place, j, p):
+    return (place[0] ^ j) * HG + ((place[1] + p) & (HG - 1))
+
+
+def token_picker():
+    row = lax.broadcasted_iota(jnp.int32, (TOK, TOK), 0)
+    col = lax.broadcasted_iota(jnp.int32, (TOK, TOK), 1)
+    return (col == RATE * (row % BLK) + row // BLK).astype(BF16)
+
+
+def fill_class_major(block, picker, scratch):
+    ordered = dot(picker, block).astype(BF16)
+    step = 256
+    eye = (
+        lax.broadcasted_iota(jnp.int32, (step, step), 0)
+        == lax.broadcasted_iota(jnp.int32, (step, step), 1)
+    ).astype(BF16)
+    for c in range(0, block.shape[1], step):
+        scratch[c : c + step, :] = dot_nt(eye, ordered[:, c : c + step]).astype(BF16)
+
+
+def lane_block(index):
+    return pl.ds(pl.multiple_of(index * BLK, BLK), BLK)
+
+
+def head_rows(head):
+    return pl.ds(pl.multiple_of(head * DH, 16), DH)
+
+
+def pack_kernel(place, mid, top, k_ref, v_ref, q_ref, *rest):
+    sel, far, scratch = rest[:GROUP], rest[GROUP : 2 * GROUP], rest[2 * GROUP :]
+    picker = token_picker()
+    for ref, held in zip((k_ref, v_ref, q_ref), scratch):
+        fill_class_major(ref[...], picker, held)
+    for j in range(GROUP):
+        for p in range(HG):
+            head = head_of(place, j, p)
+            slots = class_of_slots(mid[head], top[head])
+            for s in range(RATE):
+                out = sel[j] if s < 2 else far[j]
+                lanes = slice((s % 2) * BLK, (s % 2 + 1) * BLK)
+                for i, held in enumerate(scratch):
+                    out[p, i * DH : (i + 1) * DH, lanes] = held[
+                        head_rows(head), lane_block(slots[s])
+                    ]
+
+
+def split_query(q):
+    scaled = q.astype(F32) * (DH**-0.5 * LOG2E)
+    high = scaled.astype(BF16)
+    low = (scaled - high.astype(F32)).astype(BF16)
+    return jnp.concatenate([high, low], axis=0)
+
+
+def twice_keys(keys_t):
+    both = jnp.concatenate([keys_t, keys_t], axis=0).astype(F32)
+    return both.T.astype(BF16)
+
+
+def column_max(blocks):
+    best = jnp.max(blocks[0], axis=0, keepdims=True)
+    for block in blocks[1:]:
+        best = jnp.maximum(best, jnp.max(block, axis=0, keepdims=True))
+    return best
+
+
+def near_kernel(blocks, tasks, carried, place, mid, top, *refs):
+    kv = refs[: len(blocks)]
+    refs = refs[len(blocks) :]
+    old = [refs[2 * i : 2 * i + 2] for i in range(carried)]
+    outs = refs[2 * carried : 2 * carried + 2 * len(tasks[0])]
+    k_s, v_s = refs[-2:]
+    head = head_of(place, 0, pl.program_id(0))
+    same = (mid[head] == top[head]).astype(jnp.int32)
+    slot = lax.broadcasted_iota(jnp.int32, (1, HALF), 1) // BLK
+    first_again = jnp.where(same == 1, 1.584962500721156, 1.0)
+    second_again = jnp.where(same == 1, 0.0, 1.0)
+    again = [
+        jnp.where(slot == 0, first_again, 0.0),
+        jnp.where(slot == 1, second_again, 0.0),
+    ]
+    for i, ref in enumerate(kv):
+        rows = slice(i * HALF, (i + 1) * HALF)
+        k_s[rows, :] = twice_keys(ref[0, 0:DH, :])
+        v_s[0:DH, rows] = ref[0, DH : 2 * DH, :]
+    v_s[DH:DX, :] = jnp.ones((DX - DH, v_s.shape[1]), BF16)
+
+    flat = [
+        (block, low, merge, out, i)
+        for out, group in enumerate(tasks)
+        for i, (block, low, merge) in enumerate(group)
+    ]
+
+    def score(task):
+        block, low = task[:2]
+        return dot(k_s[low * HALF :, :], split_query(kv[blocks.index(block)][0, 2 * DH :, :]))
+
+    scores = score(flat[0])
+    for n, (block, low, merge, out, i) in enumerate(flat):
+        following = score(flat[n + 1]) if n + 1 < len(flat) else None
+        best = jnp.max(scores, axis=0, keepdims=True)
+        if merge is not None:
+            acc_in, max_in = old[merge[0]]
+            old_max = max_in[0, merge[1], 0:1, :]
+            best = jnp.maximum(best, old_max)
+        weights = []
+        for b in range(low, len(blocks)):
+            part = scores[(b - low) * HALF : (b - low + 1) * HALF, :]
+            if block[1] == 0 and blocks[b][1] == 0:
+                weights += [
+                    jnp.exp2(part[s * BLK : (s + 1) * BLK, :] - (best - again[s]))
+                    for s in range(2)
+                ]
+            else:
+                weights.append(jnp.exp2(part - best))
+        weights = jnp.concatenate([w.astype(BF16) for w in weights], axis=0)
+        acc = dot(v_s[:, low * HALF :], weights)
+        if merge is not None:
+            acc = acc + acc_in[0, merge[1]] * jnp.exp2(old_max - best)
+        acc_ref, max_ref = outs[2 * out : 2 * out + 2]
+        acc_ref[0, i] = acc
+        max_ref[0, i] = jnp.broadcast_to(best, (8, HALF))
+        scores = following
+
+
+def far_kernel(chip, place, mid, top, *refs):
+    own, beyond = refs[:GROUP], refs[GROUP : GROUP + 6]
+    outs = refs[GROUP + 6 : GROUP + 6 + RATE]
+    k_s, v_s = refs[GROUP + 6 + RATE :]
+    head = head_of(place, 0, 0)
+    same = mid[head] == top[head]
+    slots = (0, jnp.where(same, 0, 1))
+
+    def source(s, j):
+        return own[j].at[0] if s == 0 else beyond[2 * (s - 1) + j // 2].at[j % 2]
+
+    for level, slot in enumerate(slots):
+        for s in range(RATE):
+            for j in range(GROUP):
+                here = slice(j * BLK, (j + 1) * BLK)
+                ref = source(s, j)
+                k_s[level, s, here, :] = twice_keys(ref[0:DH, lane_block(slot)])
+                v_s[level, s, 0:DH, here] = ref[DH : 2 * DH, lane_block(slot)]
+    v_s[:, :, DH:DX, :] = jnp.ones((2, RATE, DX - DH, TOK), BF16)
+    row = lax.broadcasted_iota(jnp.int32, (16, HALF), 0)
+    tasks = [(s, level) for s in range(RATE) for level in range(2)]
+
+    def score(task):
+        s, level = task
+        query = jnp.concatenate(
+            [
+                split_query(source(s, 2 * chip + i)[2 * DH :, lane_block(slots[level])])
+                for i in range(2)
+            ],
+            axis=1,
+        )
+        return [dot(k_s[level, b], query) for b in range(RATE) if b != s]
+
+    scores = score(tasks[0])
+    for n, (s, level) in enumerate(tasks):
+        following = score(tasks[n + 1]) if n + 1 < len(tasks) else None
+        best = column_max(scores)
+        acc = None
+        for i, b in enumerate([b for b in range(RATE) if b != s]):
+            part = dot(v_s[level, b], jnp.exp2(scores[i] - best).astype(BF16))
+            acc = part if acc is None else acc + part
+        total = acc[DH : DH + 1, :]
+        result = (acc[0:DH, :] / total).astype(BF16)
+        lse = best + jnp.log2(total)
+        if level == 0:
+            lse = jnp.where(same, lse + 1.0, lse)
+        else:
+            lse = jnp.where(same, -1e30, lse)
+        high = lse.astype(BF16).astype(F32)
+        middle = (lse - high).astype(BF16).astype(F32)
+        low = lse - high - middle
+        tail = jnp.where(row == 0, high, jnp.where(row == 1, middle, jnp.where(row == 2, low, 0.0)))
+        tail = tail.astype(BF16)
+        for i in range(2):
+            lanes = slice(i * HALF + level * BLK, i * HALF + (level + 1) * BLK)
+            outs[s][0:DH, lanes] = result[:, i * BLK : (i + 1) * BLK]
+            outs[s][DH:DX, lanes] = tail[:, i * BLK : (i + 1) * BLK]
+        scores = following
+
+
+def combine_kernel(acc_ref, max_ref, *refs):
+    far, outs = refs[:HG], refs[HG:]
+    for p in range(HG):
+        for i in range(2):
+            lanes = slice(i * HALF, (i + 1) * HALF)
+            acc, best = acc_ref[p, 2 * i], max_ref[p, 2 * i, 0:1, :]
+            tail = far[p][DH:DX, lanes].astype(F32)
+            lse = tail[0:1] + tail[1:2] + tail[2:3]
+            overall = jnp.maximum(best, lse)
+            near_factor, far_factor = jnp.exp2(best - overall), jnp.exp2(lse - overall)
+            total = acc[DH : DH + 1] * near_factor + far_factor
+            value = acc[0:DH] * near_factor + far[p][0:DH, lanes].astype(F32) * far_factor
+            outs[i][p, :, 0:HALF] = (value / total).astype(BF16)
+            acc = acc_ref[p, 2 * i + 1]
+            outs[i][p, :, HALF:] = (acc[0:DH] / acc[DH : DH + 1]).astype(BF16)
+
+
+def project_kernel(place, mid, top, *refs):
+    parts = refs[:GROUP]
+    w_ref, out_ref, held = refs[GROUP:]
+    for j in range(GROUP):
+        for p in range(HG):
+            head = head_of(place, j, p)
+            slots = class_of_slots(mid[head], top[head])
+            for s in range(RATE):
+                held[head_rows(head), lane_block(slots[s])] = parts[j][
+                    p, :, s * BLK : (s + 1) * BLK
+                ]
+    row = lax.broadcasted_iota(jnp.int32, (TOK, TOK), 0)
+    col = lax.broadcasted_iota(jnp.int32, (TOK, TOK), 1)
+    picker = (row == RATE * (col % BLK) + col // BLK).astype(BF16)
+    attention = dot_nt(picker, held[...]).astype(BF16)
+    out_ref[...] = dot(attention, w_ref[...]).astype(BF16)
+
+
+def whole(shape):
+    return pl.BlockSpec(shape, lambda *_: (0,) * len(shape))
+
+
+def per_head(shape):
+    return pl.BlockSpec(shape, lambda h, *_: (h,) + (0,) * (len(shape) - 1))
+
+
+def call(kernel, scalars, args, grid, in_specs, outs, scratch, scores, limit=VMEM_LIMIT):
+    return pl.pallas_call(
+        kernel,
+        grid_spec=pltpu.PrefetchScalarGridSpec(
+            num_scalar_prefetch=len(scalars),
+            grid=grid,
+            in_specs=in_specs,
+            out_specs=[spec for spec, _ in outs],
+            scratch_shapes=scratch,
+        ),
+        out_shape=[shape for _, shape in outs],
+        compiler_params=pltpu.CompilerParams(vmem_limit_bytes=limit),
+        cost_estimate=pl.CostEstimate(
+            flops=scores * 1024, bytes_accessed=1 << 20, transcendentals=scores
+        ),
+    )(*scalars, *args)
+
+
+def within(array, apart):
+    count = lax.axis_size("seq")
+    return lax.ppermute(array, "seq", [(i, i ^ apart) for i in range(count)])
+
+
+def across(array, segments):
+    count = lax.axis_size("seq")
+    return lax.ppermute(
+        array, "seq", [(i, (i + GROUP * segments) % count) for i in range(count)]
+    )
+
+
+def shards_four(queries, key_states, value_states, offsets_mid, offsets_top, out_weight):
+    width = queries.shape[1]
+    index = lax.axis_index("seq").astype(jnp.int32)
+    place = jnp.stack([index % GROUP, index // GROUP])
+    scalars = (place, offsets_mid, offsets_top)
+    piece = jax.ShapeDtypeStruct((HG, 3 * DH, HALF), BF16)
+    packed = call(
+        pack_kernel, scalars, (key_states, value_states, queries), (1,),
+        [whole((TOK, width))] * 3,
+        [(whole(piece.shape), piece)] * (2 * GROUP),
+        [pltpu.VMEM((width, TOK), BF16)] * 3,
+        1 << 19, VMEM_MOST,
+    )
+    sel, rest = list(packed[:GROUP]), list(packed[GROUP:])
+    sel[1] = within(sel[1], 1)
+    rest[1] = within(rest[1], 1)
+    for j in (2, 3):
+        sel[j] = within(sel[j], j)
+    for j in (2, 3):
+        rest[j] = within(rest[j], j)
+
+    beyond = []
+    for s in range(1, RATE):
+        beyond += [
+            across(jnp.stack([sel[0][s], sel[1][s]]), s),
+            across(jnp.stack([sel[2][s], sel[3][s]]), s),
+        ]
+
+    piece_spec = per_head((1, 3 * DH, HALF))
+
+    def state(count):
+        return [
+            (per_head((1, count, rows, HALF)), jax.ShapeDtypeStruct((HG, count, rows, HALF), F32))
+            for rows in (DX, 8)
+        ]
+
+    held = {(j, half): (sel, rest)[half][j] for j in range(GROUP) for half in range(2)}
+
+    def near(blocks, tasks, old):
+        keys = len(blocks) * HALF
+        scores = sum((len(blocks) - low) * HALF * HALF for group in tasks for _, low, _ in group)
+        return call(
+            functools.partial(near_kernel, blocks, tasks, len(old)), scalars,
+            (*[held[b] for b in blocks], *[x for pair in old for x in pair]), (HG,),
+            [piece_spec] * len(blocks)
+            + [per_head((1,) + x.shape[1:]) for pair in old for x in pair],
+            [out for group in tasks for out in state(len(group))],
+            [pltpu.VMEM((keys, 2 * DH), BF16), pltpu.VMEM((DX, keys), BF16)],
+            HG * scores,
+        )
+
+    own = [(0, 0), (0, 1), (1, 0), (1, 1)]
+    state_own = near(own, [[(b, 0, None) for b in own]], [])
+    with_sel = own + [(2, 0), (3, 0)]
+    out = near(
+        with_sel,
+        [
+            [(b, 4, (0, i)) for i, b in enumerate(own)],
+            [((2, 0), 0, None), ((3, 0), 0, None)],
+        ],
+        [state_own],
+    )
+    state_own, state_sel = out[:2], out[2:]
+
+    piece_0 = pl.BlockSpec((1, 3 * DH, HALF), lambda *_: (0, 0, 0))
+    result = jax.ShapeDtypeStruct((DX, 2 * HALF), BF16)
+
+    def far(chip):
+        return call(
+            functools.partial(far_kernel, chip), scalars, (*sel, *beyond), (1,),
+            [piece_0] * GROUP + [whole((2, 3 * DH, HALF))] * 6,
+            [(whole(result.shape), result)] * RATE,
+            [
+                pltpu.VMEM((2, RATE, TOK, 2 * DH), BF16),
+                pltpu.VMEM((2, RATE, DX, TOK), BF16),
+            ],
+            RATE * 2 * 3 * TOK * HALF,
+        )
+
+    back = {}
+    for chip in (1, 0):
+        results = far(chip)
+        back[chip] = [results[0]] + [across(results[s], -s) for s in range(1, RATE)]
+
+    everything = with_sel + [(2, 1), (3, 1)]
+    out = near(
+        everything,
+        [
+            [(b, 6, (0, i)) for i, b in enumerate(own)],
+            [
+                ((2, 0), 6, (1, 0)), ((2, 1), 0, None),
+                ((3, 0), 6, (1, 1)), ((3, 1), 0, None),
+            ],
+        ],
+        [state_own, state_sel],
+    )
+    attended = jax.ShapeDtypeStruct((HG, DH, TOK), BF16)
+
+    def combine(state, results):
+        return call(
+            combine_kernel, (), (*state, *results), (1,),
+            [whole(x.shape) for x in state] + [whole(result.shape)] * HG,
+            [(whole(attended.shape), attended)] * 2,
+            [],
+            1 << 18,
+        )
+
+    parts = [None] * GROUP
+    parts[2:] = combine(out[2:], back[1])
+    parts[:2] = combine(out[:2], back[0])
+    for j in (2, 3, 1):
+        parts[j] = within(parts[j], j)
+    return call(
+        project_kernel, scalars, (*parts, out_weight), (1,),
+        [whole(attended.shape)] * GROUP + [whole((width, width))],
+        [(whole((TOK, width)), jax.ShapeDtypeStruct((TOK, width), BF16))],
+        [pltpu.VMEM((width, TOK), BF16)],
+        1 << 18,
+    )[0]
+
+
+def shards(queries, key_states, value_states, offsets_mid, offsets_top, out_weight):
+    tokens, width = queries.shape
+    heads = offsets_mid.shape[0]
+    fits = (
+        lax.axis_size("head") == 1
+        and lax.axis_size("seq") == GROUP * RATE
+        and tokens == TOK
+        and heads == GROUP * HG
+        and width == heads * DH
+    )
+    run = shards_four if fits else shards_general
+    return run(queries, key_states, value_states, offsets_mid, offsets_top, out_weight)
+
+
 def solution(mesh):
     in_specs = (
         P(("slide", "seq"), "head"),

time: 421 us -> 97.6 us (0.23)
  matrix products: 147 us -> 0 us
  local copies, waits for them, and re-layouts: 115 us -> 1.06 us
  other arithmetic: 62.4 us -> 0.76 us
  Pallas kernels: 0 us -> 51.2 us
  waiting for transfers between devices: 70.3 us -> 19.6 us
  starting transfers between devices: 7.97 us -> 24.5 us
  between operations: 13.8 us -> 0.31 us
    dot_general x99 -> x0, matrix products: 147 us -> none  [the longest x48 71.2 us: attend_head(): numerator = jnp.dot(weights, value_rows, preferred_element_type=jnp.float32)]
    pallas_call x0 -> x9, Pallas kernels: none -> 51.2 us  [call(): pl.pallas_call(kernel, grid_spec=pltpu.PrefetchScalarGridSpec(num_scalar_...]
    ppermute x6 -> x21, waiting for transfers between devices: 70.2 us -> 19.6 us  [the longest x9 19.6 us: within(): return lax.ppermute(array, 'seq', [(i, i ^ apart) for i in range(count)])]
    dynamic_update_slice x96 -> x0, local copies, waits for them, and re-layouts: 45 us -> none  [attend_local(): lax.map(attend_head, (query_rows.transpose(1, 0, 2), pair_rows[:, 0].tran...]
    select_n x10 -> x0, other arithmetic: 32.3 us -> none  [doubling(): jnp.where(is_lower, jnp.concatenate([buffer, partner], 0), jnp.concatenat...]
    broadcast_in_dim x18 -> x0, local copies, waits for them, and re-layouts: 23.3 us -> none  [the longest x6 20.3 us: spread_back(): jnp.where(chosen[None, :, :, None], numerator.transpose(1, 0, 2)[:, None]...]
    reduce_sum x48 -> x0, other arithmetic: 22.5 us -> none  [attend_head(): row_total = jnp.sum(shifted, axis=1)]
    another operation x11 -> x0, local copies, waits for them, and re-layouts: 17.6 us -> none  [the longest x4 13.9 us: shards(): jnp.stack([key_states, value_states], axis=1)]
  transfers between devices with their start and end apart: 7 -> 21, of which waited for: 5 -> 3; matrix products, arithmetic and copies ran while one was open for 59% -> 1% of each run, Pallas kernels for 0% -> 43%
where the time goes in v1:
time: 97.6 us; the launch traced here: 97.4 us
  Pallas kernels  51.2 us (52%)
  starting transfers between devices  24.5 us (25%)
  waiting for transfers between devices  19.6 us (20%)
  local copies, waits for them, and re-layouts  1.06 us (1%)
    pallas_call x9, Pallas kernels, call(): pl.pallas_call(kernel, grid_spec=pltpu.PrefetchScalarGridSpec(num_scalar_...  51.2 us
    ppermute x9, waiting for transfers between devices, within(): return lax.ppermute(array, 'seq', [(i, i ^ apart) for i in range(count)])  19.6 us
    ppermute x12, starting transfers between devices, across(): lax.ppermute(array, 'seq', [(i, (i + GROUP * segments) % count) for i in...  17.6 us
    ppermute x9, starting transfers between devices, within(): return lax.ppermute(array, 'seq', [(i, i ^ apart) for i in range(count)])  6.88 us
  transfers between devices with their start and end apart: 21, of which 3 were waited for; matrix products, arithmetic and copies ran while one was open for 1% of the time, Pallas kernels for 43%

profile of v1, /device:TPU:0, one launch (start us, length us, event | category | flops | bytes accessed | tf_op | source)
XLA Modules:
  0.0 97.4 jit_solution(3752940597555590086)
XLA Ops:
  0.0 0.7 pad_add_fusion.place
  0.7 6.1 %shard_map.64 = (bf16[4,144,256]{2,1,0:T(8,128)(2,1)}, bf16[4,144,256]{2,1,0:T(8,128)(2,1)}, bf16[4,144,256]{2,1,0:T(8,128)(2,1)}, bf16[4,144,256]{2,1,0:T(8,128...) custom-call(s32[2]{0:T(128)} %pad_add_fusion.place, ...), custom_call_target="tpu_custom_call" | custom-call | flops 536870912 | bytes 1048576 | tf_op jit(solution)/shard_map/pallas_call | solution.py:402
  6.8 0.4 collective-permute-start
  7.3 2.9 %collective-permute-start.2 = (bf16[4,144,256]{2,1,0:T(8,128)(2,1)}, bf16[4,144,256]{2,1,0:T(8,128)(2,1)S(1)}, u32[]{:S(2)}, u32[]{:S(2)}) collective-permute-start(bf16[4,144,256]{2,1,0:T(8,128)(2,1)} %get-tuple-element.39), channel_id=1, source_target_pairs={{0,2},{1,3},{2,0},{3,1},{4,6},{5,7},{6,4},{7,5},{8,10},{9,11},{10,... | collective-permute-start | bytes 884744 | tf_op jit(solution)/shard_map/ppermute | solution.py:421
  10.2 1.0 fusion.2
  11.3 1.6 %collective-permute-start.6 = (bf16[2,144,256]{2,1,0:T(8,128)(2,1)S(1)}, bf16[2,144,256]{2,1,0:T(8,128)(2,1)S(1)}, u32[]{:S(2)}, u32[]{:S(2)}) collective-permute-start(bf16[2,144,256]{2,1,0:T(8,128)(2,1)S(1)} %pad_maximum_fusion), channel_id=1, source_target_pairs={{0,4},{1,5},{2,6},{3,7},{4,8},{5,9},{6,10},{7,11},{8,12},{9,13},{1... | collective-permute-start | bytes 442376 | tf_op jit(solution)/shard_map/ppermute | solution.py:426
  12.9 10.3 %collective-permute-done.3.refs_5_.refs_3_ = bf16[4,144,256]{2,1,0:T(8,128)(2,1)S(1)} collective-permute-done((bf16[4,144,256]{2,1,0:T(8,128)(2,1)}, bf16[4,144,256]{2,1,0:T(8,128)(2,1)S(1)}, u32[]{:S(2)}, u32[]{:S(2)}) %collective-permute-start.3) | collective-permute-done | bytes 294944 | tf_op jit(solution)/shard_map/ppermute | solution.py:421
  23.3 1.6 %collective-permute-start.7 = (bf16[2,144,256]{2,1,0:T(8,128)(2,1)S(1)}, bf16[2,144,256]{2,1,0:T(8,128)(2,1)S(1)}, u32[]{:S(2)}, u32[]{:S(2)}) collective-permute-start(bf16[2,144,256]{2,1,0:T(8,128)(2,1)S(1)} %pad_maximum_fusion.1), channel_id=1, source_target_pairs={{0,4},{1,5},{2,6},{3,7},{4,8},{5,9},{6,10},{7,11},{8,12},{9,13},{1... | collective-permute-start | bytes 442376 | tf_op jit(solution)/shard_map/ppermute | solution.py:426
  25.0 2.7 %collective-permute-start.8 = (bf16[2,144,256]{2,1,0:T(8,128)(2,1)S(1)}, bf16[2,144,256]{2,1,0:T(8,128)(2,1)S(1)}, u32[]{:S(2)}, u32[]{:S(2)}) collective-permute-start(bf16[2,144,256]{2,1,0:T(8,128)(2,1)S(1)} %pad_maximum_fusion.2), channel_id=1, source_target_pairs={{0,8},{1,9},{2,10},{3,11},{4,12},{5,13},{6,14},{7,15},{8,0},{9,1},... | collective-permute-start | bytes 442376 | tf_op jit(solution)/shard_map/ppermute | solution.py:426
  27.7 0.4 collective-permute-start.9
  28.1 2.3 %collective-permute-start.10 = (bf16[2,144,256]{2,1,0:T(8,128)(2,1)S(1)}, bf16[2,144,256]{2,1,0:T(8,128)(2,1)S(1)}, u32[]{:S(2)}, u32[]{:S(2)}) collective-permute-start(bf16[2,144,256]{2,1,0:T(8,128)(2,1)S(1)} %pad_maximum_fusion.4), channel_id=1, source_target_pairs={{0,12},{1,13},{2,14},{3,15},{4,0},{5,1},{6,2},{7,3},{8,4},{9,5},{1... | collective-permute-start | bytes 442376 | tf_op jit(solution)/shard_map/ppermute | solution.py:426
  30.4 8.2 %shard_map.65 = (f32[4,4,64,256]{3,2,1,0:T(8,128)S(1)}, f32[4,4,8,256]{3,2,1,0:T(8,128)S(1)}) custom-call(s32[2]{0:T(128)S(1)} %copy-done.4, s32[16]{0:T(128)S(1)} %copy-done.2, s32[16]{0:T(128)S(1)} %copy-done.3, bf16[4,144,256]{2,1,0:T(8,128)(2,1)S(1)} %copy-done.1, bf16[4,144,256]{2,1,0:T(8,128)(2,1)S(1)} %copy-done.5, ...), custom_call_target="tpu_custom_call" | custom-call | flops 4294967296 | bytes 1048576 | tf_op jit(solution)/shard_map/pallas_call | solution.py:402
  38.7 1.9 %collective-permute-start.11 = (bf16[2,144,256]{2,1,0:T(8,128)(2,1)S(1)}, bf16[2,144,256]{2,1,0:T(8,128)(2,1)S(1)}, u32[]{:S(2)}, u32[]{:S(2)}) collective-permute-start(bf16[2,144,256]{2,1,0:T(8,128)(2,1)S(1)} %pad_maximum_fusion.5), channel_id=1, source_target_pairs={{0,12},{1,13},{2,14},{3,15},{4,0},{5,1},{6,2},{7,3},{8,4},{9,5},{1... | collective-permute-start | bytes 442376 | tf_op jit(solution)/shard_map/ppermute | solution.py:426
  40.5 9.2 %shard_map.66 = (f32[4,4,64,256]{3,2,1,0:T(8,128)S(1)}, f32[4,4,8,256]{3,2,1,0:T(8,128)S(1)}, f32[4,2,64,256]{3,2,1,0:T(8,128)S(1)}, f32[4,2,8,256]{3,2,1,0:T(8,128)S(1)}) custom-call(s32[2]{0:T(128)S(1)} %copy-done.4, s32[16]{0:T(128)S(1)} %copy-done.2, s32[16]{0:T(128)S(1)} %copy-done.3, bf16[4,144,256]{2,1,0:T(8,128)(2,1)S(1)} %copy-done.1, ...), custom_call_target="tpu_custom_call" | custom-call | flops 5368709120 | bytes 1048576 | tf_op jit(solution)/shard_map/pallas_call | solution.py:402
  49.8 1.5 %collective-permute-start.4 = (bf16[4,144,256]{2,1,0:T(8,128)(2,1)S(1)}, bf16[4,144,256]{2,1,0:T(8,128)(2,1)S(1)}, u32[]{:S(2)}, u32[]{:S(2)}) collective-permute-start(bf16[4,144,256]{2,1,0:T(8,128)(2,1)S(1)} %copy-done.7), channel_id=1, source_target_pairs={{0,2},{1,3},{2,0},{3,1},{4,6},{5,7},{6,4},{7,5},{8,10},{9,11},{10,... | collective-permute-start | bytes 884744 | tf_op jit(solution)/shard_map/ppermute | solution.py:421
  51.3 4.7 %shard_map.68 = (bf16[64,512]{1,0:T(8,128)(2,1)S(1)}, bf16[64,512]{1,0:T(8,128)(2,1)S(1)}, bf16[64,512]{1,0:T(8,128)(2,1)S(1)}, bf16[64,512]{1,0:T(8,128)(2,1)S(1)}) custom-call(s32[2]{0:T(128)S(1)} %copy-done.4, s32[16]{0:T(128)S(1)} %copy-done.2, s32[16]{0:T(128)S(1)} %copy-done.3, bf16[4,144,256]{2,1,0:T(8,128)(2,1)S(1)} %copy-done.1, ...), custom_call_target="tpu_custom_call" | custom-call | flops 3221225472 | bytes 1048576 | tf_op jit(solution)/shard_map/pallas_call | solution.py:402
  56.0 1.1 %collective-permute-start.12 = (bf16[64,512]{1,0:T(8,128)(2,1)S(1)}, bf16[64,512]{1,0:T(8,128)(2,1)S(1)}, u32[]{:S(2)}, u32[]{:S(2)}) collective-permute-start(bf16[64,512]{1,0:T(8,128)(2,1)S(1)} %get-tuple-element.52), channel_id=1, source_target_pairs={{0,12},{1,13},{2,14},{3,15},{4,0},{5,1},{6,2},{7,3},{8,4},{9,5},{1... | collective-permute-start | bytes 196616 | tf_op jit(solution)/shard_map/ppermute | solution.py:426
  57.0 0.6 collective-permute-start.13
  57.7 0.4 collective-permute-start.14
  58.0 4.6 %shard_map.70 = (bf16[64,512]{1,0:T(8,128)(2,1)S(1)}, bf16[64,512]{1,0:T(8,128)(2,1)S(1)}, bf16[64,512]{1,0:T(8,128)(2,1)S(1)}, bf16[64,512]{1,0:T(8,128)(2,1)S(1)}) custom-call(s32[2]{0:T(128)S(1)} %copy-done.4, s32[16]{0:T(128)S(1)} %copy-done.2, s32[16]{0:T(128)S(1)} %copy-done.3, bf16[4,144,256]{2,1,0:T(8,128)(2,1)S(1)} %copy-done.1, ...), custom_call_target="tpu_custom_call" | custom-call | flops 3221225472 | bytes 1048576 | tf_op jit(solution)/shard_map/pallas_call | solution.py:402
  62.7 3.5 %collective-permute-start.16 = (bf16[64,512]{1,0:T(8,128)(2,1)S(1)}, bf16[64,512]{1,0:T(8,128)(2,1)S(1)}, u32[]{:S(2)}, u32[]{:S(2)}) collective-permute-start(bf16[64,512]{1,0:T(8,128)(2,1)S(1)} %get-tuple-element.60), channel_id=1, source_target_pairs={{0,12},{1,13},{2,14},{3,15},{4,0},{5,1},{6,2},{7,3},{8,4},{9,5},{1... | collective-permute-start | bytes 196616 | tf_op jit(solution)/shard_map/ppermute | solution.py:426
  66.2 0.5 collective-permute-start.17
  66.7 1.0 %collective-permute-start.18 = (bf16[64,512]{1,0:T(8,128)(2,1)S(1)}, bf16[64,512]{1,0:T(8,128)(2,1)S(1)}, u32[]{:S(2)}, u32[]{:S(2)}) collective-permute-start(bf16[64,512]{1,0:T(8,128)(2,1)S(1)} %get-tuple-element.62), channel_id=1, source_target_pairs={{0,4},{1,5},{2,6},{3,7},{4,8},{5,9},{6,10},{7,11},{8,12},{9,13},{1... | collective-permute-start | bytes 196616 | tf_op jit(solution)/shard_map/ppermute | solution.py:426
  67.7 15.1 %shard_map.67 = (f32[4,4,64,256]{3,2,1,0:T(8,128)S(1)}, f32[4,4,8,256]{3,2,1,0:T(8,128)S(1)}, f32[4,4,64,256]{3,2,1,0:T(8,128)S(1)}, f32[4,4,8,256]{3,2,1,0:T(8,128)S(1)}) custom-call(s32[2]{0:T(128)S(1)} %copy-done.4, s32[16]{0:T(128)S(1)} %copy-done.2, s32[16]{0:T(128)S(1)} %copy-done.3, bf16[4,144,256]{2,1,0:T(8,128)(2,1)S(1)} %copy-done.1, ...), custom_call_target="tpu_custom_call" | custom-call | flops 7516192768 | bytes 1048576 | tf_op jit(solution)/shard_map/pallas_call | solution.py:402
  82.9 0.1 shard_map.69
  83.0 0.1 collective-permute-start.15
  83.1 0.1 shard_map.71
  83.3 0.8 collective-permute-start.19
  84.1 1.1 %collective-permute-start.20 = (bf16[4,48,512]{2,1,0:T(8,128)(2,1)S(1)}, bf16[4,48,512]{2,1,0:T(8,128)(2,1)S(1)}, u32[]{:S(2)}, u32[]{:S(2)}) collective-permute-start(bf16[4,48,512]{2,1,0:T(8,128)(2,1)S(1)} %get-tuple-element.64), channel_id=1, source_target_pairs={{0,3},{1,2},{2,1},{3,0},{4,7},{5,6},{6,5},{7,4},{8,11},{9,10},{10,... | collective-permute-start | bytes 589832 | tf_op jit(solution)/shard_map/ppermute | solution.py:421
  85.2 5.9 %collective-permute-done.19.refs_2_ = bf16[4,48,512]{2,1,0:T(8,128)(2,1)S(1)} collective-permute-done((bf16[4,48,512]{2,1,0:T(8,128)(2,1)S(1)}, bf16[4,48,512]{2,1,0:T(8,128)(2,1)S(1)}, u32[]{:S(2)}, u32[]{:S(2)}) %collective-permute-start.19) | collective-permute-done | bytes 196640 | tf_op jit(solution)/shard_map/ppermute | solution.py:421
  91.0 3.4 %collective-permute-done.20.refs_3_ = bf16[4,48,512]{2,1,0:T(8,128)(2,1)S(1)} collective-permute-done((bf16[4,48,512]{2,1,0:T(8,128)(2,1)S(1)}, bf16[4,48,512]{2,1,0:T(8,128)(2,1)S(1)}, u32[]{:S(2)}, u32[]{:S(2)}) %collective-permute-start.20) | collective-permute-done | bytes 196640 | tf_op jit(solution)/shard_map/ppermute | solution.py:421
  94.4 3.0 %shard_map.72 = bf16[512,768]{1,0:T(8,128)(2,1)} custom-call(s32[2]{0:T(128)S(1)} %copy-done.4, s32[16]{0:T(128)S(1)} %copy-done.2, s32[16]{0:T(128)S(1)} %copy-done.3, bf16[4,48,512]{2,1,0:T(8,128)(2,1)S(1)} %get-tuple-element.55.refs_0_, bf16[4,48,512]{2,1,0:T(8,128)(2,1)S(1)} %collective-permute-done.15.refs_1_, ...), custom_call_target="tpu_custom_call" | custom-call | flops 268435456 | bytes 1048576 | tf_op jit(solution)/shard_map/pallas_call | solution.py:402
  (46 shorter events, 0.3 us)
Async XLA Ops:
  6.8 4.4 %collective-permute-start = (bf16[4,144,256]{2,1,0:T(8,128)(2,1)}, bf16[4,144,256]{2,1,0:T(8,128)(2,1)S(1)}, u32[]{:S(2)}, u32[]{:S(2)}) collective-permute-start(bf16[4,144,256]{2,1,0:T(8,128)(2,1)} %get-tuple-element.37), channel_id=1, source_target_pairs={{0,1},{1,0},{2,3},{3,2},{4,5},{5,4},{6,7},{7,6},{8,9},{9,8},{10,11... | collective-permute-start | bytes 884744 | tf_op jit(solution)/shard_map/ppermute | solution.py:421
  7.2 20.9 %collective-permute-start.1 = (bf16[4,144,256]{2,1,0:T(8,128)(2,1)}, bf16[4,144,256]{2,1,0:T(8,128)(2,1)S(1)}, u32[]{:S(2)}, u32[]{:S(2)}) collective-permute-start(bf16[4,144,256]{2,1,0:T(8,128)(2,1)} %get-tuple-element.38), channel_id=1, source_target_pairs={{0,1},{1,0},{2,3},{3,2},{4,5},{5,4},{6,7},{7,6},{8,9},{9,8},{10,11... | collective-permute-start | bytes 884744 | tf_op jit(solution)/shard_map/ppermute | solution.py:421
  7.3 16.0 %collective-permute-start.2 = (bf16[4,144,256]{2,1,0:T(8,128)(2,1)}, bf16[4,144,256]{2,1,0:T(8,128)(2,1)S(1)}, u32[]{:S(2)}, u32[]{:S(2)}) collective-permute-start(bf16[4,144,256]{2,1,0:T(8,128)(2,1)} %get-tuple-element.39), channel_id=1, source_target_pairs={{0,2},{1,3},{2,0},{3,1},{4,6},{5,7},{6,4},{7,5},{8,10},{9,11},{10,... | collective-permute-start | bytes 884744 | tf_op jit(solution)/shard_map/ppermute | solution.py:421
  10.2 13.1 %collective-permute-start.3 = (bf16[4,144,256]{2,1,0:T(8,128)(2,1)}, bf16[4,144,256]{2,1,0:T(8,128)(2,1)S(1)}, u32[]{:S(2)}, u32[]{:S(2)}) collective-permute-start(bf16[4,144,256]{2,1,0:T(8,128)(2,1)} %get-tuple-element.40), channel_id=1, source_target_pairs={{0,3},{1,2},{2,1},{3,0},{4,7},{5,6},{6,5},{7,4},{8,11},{9,10},{10,... | collective-permute-start | bytes 884744 | tf_op jit(solution)/shard_map/ppermute | solution.py:421
  11.2 19.2 %copy-start.1 = (bf16[4,144,256]{2,1,0:T(8,128)(2,1)S(1)}, bf16[4,144,256]{2,1,0:T(8,128)(2,1)}, u32[]{:S(2)}) copy-start(bf16[4,144,256]{2,1,0:T(8,128)(2,1)} %get-tuple-element.35.refs_0_) | copy-start | bytes 884740
  11.2 19.2 %copy-start.2 = (s32[16]{0:T(128)S(1)}, s32[16]{0:T(128)}, u32[]{:S(2)}) copy-start(s32[16]{0:T(128)} %mid.13) | copy-start | bytes 196
  11.2 19.2 %copy-start.3 = (s32[16]{0:T(128)S(1)}, s32[16]{0:T(128)}, u32[]{:S(2)}) copy-start(s32[16]{0:T(128)} %top.13) | copy-start | bytes 196
  11.2 19.2 %copy-start.4 = (s32[2]{0:T(128)S(1)}, s32[2]{0:T(128)}, u32[]{:S(2)}) copy-start(s32[2]{0:T(128)} %pad_add_fusion.place) | copy-start | bytes 28
  11.3 19.2 %copy-start.5 = (bf16[4,144,256]{2,1,0:T(8,128)(2,1)S(1)}, bf16[4,144,256]{2,1,0:T(8,128)(2,1)}, u32[]{:S(2)}) copy-start(bf16[4,144,256]{2,1,0:T(8,128)(2,1)} %get-tuple-element.36.refs_1_) | copy-start | bytes 884740
  11.3 27.4 %collective-permute-start.6 = (bf16[2,144,256]{2,1,0:T(8,128)(2,1)S(1)}, bf16[2,144,256]{2,1,0:T(8,128)(2,1)S(1)}, u32[]{:S(2)}, u32[]{:S(2)}) collective-permute-start(bf16[2,144,256]{2,1,0:T(8,128)(2,1)S(1)} %pad_maximum_fusion), channel_id=1, source_target_pairs={{0,4},{1,5},{2,6},{3,7},{4,8},{5,9},{6,10},{7,11},{8,12},{9,13},{1... | collective-permute-start | bytes 442376 | tf_op jit(solution)/shard_map/ppermute | solution.py:426
  23.3 26.4 %collective-permute-start.7 = (bf16[2,144,256]{2,1,0:T(8,128)(2,1)S(1)}, bf16[2,144,256]{2,1,0:T(8,128)(2,1)S(1)}, u32[]{:S(2)}, u32[]{:S(2)}) collective-permute-start(bf16[2,144,256]{2,1,0:T(8,128)(2,1)S(1)} %pad_maximum_fusion.1), channel_id=1, source_target_pairs={{0,4},{1,5},{2,6},{3,7},{4,8},{5,9},{6,10},{7,11},{8,12},{9,13},{1... | collective-permute-start | bytes 442376 | tf_op jit(solution)/shard_map/ppermute | solution.py:426
  25.0 26.2 %collective-permute-start.8 = (bf16[2,144,256]{2,1,0:T(8,128)(2,1)S(1)}, bf16[2,144,256]{2,1,0:T(8,128)(2,1)S(1)}, u32[]{:S(2)}, u32[]{:S(2)}) collective-permute-start(bf16[2,144,256]{2,1,0:T(8,128)(2,1)S(1)} %pad_maximum_fusion.2), channel_id=1, source_target_pairs={{0,8},{1,9},{2,10},{3,11},{4,12},{5,13},{6,14},{7,15},{8,0},{9,1},... | collective-permute-start | bytes 442376 | tf_op jit(solution)/shard_map/ppermute | solution.py:426
  27.7 23.6 %collective-permute-start.9 = (bf16[2,144,256]{2,1,0:T(8,128)(2,1)S(1)}, bf16[2,144,256]{2,1,0:T(8,128)(2,1)S(1)}, u32[]{:S(2)}, u32[]{:S(2)}) collective-permute-start(bf16[2,144,256]{2,1,0:T(8,128)(2,1)S(1)} %pad_maximum_fusion.3), channel_id=1, source_target_pairs={{0,8},{1,9},{2,10},{3,11},{4,12},{5,13},{6,14},{7,15},{8,0},{9,1},... | collective-permute-start | bytes 442376 | tf_op jit(solution)/shard_map/ppermute | solution.py:426
  28.1 23.2 %collective-permute-start.10 = (bf16[2,144,256]{2,1,0:T(8,128)(2,1)S(1)}, bf16[2,144,256]{2,1,0:T(8,128)(2,1)S(1)}, u32[]{:S(2)}, u32[]{:S(2)}) collective-permute-start(bf16[2,144,256]{2,1,0:T(8,128)(2,1)S(1)} %pad_maximum_fusion.4), channel_id=1, source_target_pairs={{0,12},{1,13},{2,14},{3,15},{4,0},{5,1},{6,2},{7,3},{8,4},{9,5},{1... | collective-permute-start | bytes 442376 | tf_op jit(solution)/shard_map/ppermute | solution.py:426
  38.7 12.6 %collective-permute-start.11 = (bf16[2,144,256]{2,1,0:T(8,128)(2,1)S(1)}, bf16[2,144,256]{2,1,0:T(8,128)(2,1)S(1)}, u32[]{:S(2)}, u32[]{:S(2)}) collective-permute-start(bf16[2,144,256]{2,1,0:T(8,128)(2,1)S(1)} %pad_maximum_fusion.5), channel_id=1, source_target_pairs={{0,12},{1,13},{2,14},{3,15},{4,0},{5,1},{6,2},{7,3},{8,4},{9,5},{1... | collective-permute-start | bytes 442376 | tf_op jit(solution)/shard_map/ppermute | solution.py:426
  40.5 9.2 %copy-start.7 = (bf16[4,144,256]{2,1,0:T(8,128)(2,1)S(1)}, bf16[4,144,256]{2,1,0:T(8,128)(2,1)}, u32[]{:S(2)}) copy-start(bf16[4,144,256]{2,1,0:T(8,128)(2,1)} %get-tuple-element.41) | copy-start | bytes 884740
  40.5 10.7 %copy-start.6 = (bf16[4,144,256]{2,1,0:T(8,128)(2,1)S(1)}, bf16[4,144,256]{2,1,0:T(8,128)(2,1)}, u32[]{:S(2)}) copy-start(bf16[4,144,256]{2,1,0:T(8,128)(2,1)} %get-tuple-element.42) | copy-start | bytes 884740
  49.8 12.9 %collective-permute-start.4 = (bf16[4,144,256]{2,1,0:T(8,128)(2,1)S(1)}, bf16[4,144,256]{2,1,0:T(8,128)(2,1)S(1)}, u32[]{:S(2)}, u32[]{:S(2)}) collective-permute-start(bf16[4,144,256]{2,1,0:T(8,128)(2,1)S(1)} %copy-done.7), channel_id=1, source_target_pairs={{0,2},{1,3},{2,0},{3,1},{4,6},{5,7},{6,4},{7,5},{8,10},{9,11},{10,... | collective-permute-start | bytes 884744 | tf_op jit(solution)/shard_map/ppermute | solution.py:421
  51.2 15.0 %collective-permute-start.5 = (bf16[4,144,256]{2,1,0:T(8,128)(2,1)S(1)}, bf16[4,144,256]{2,1,0:T(8,128)(2,1)S(1)}, u32[]{:S(2)}, u32[]{:S(2)}) collective-permute-start(bf16[4,144,256]{2,1,0:T(8,128)(2,1)S(1)} %copy-done.6), channel_id=1, source_target_pairs={{0,3},{1,2},{2,1},{3,0},{4,7},{5,6},{6,5},{7,4},{8,11},{9,10},{10,... | collective-permute-start | bytes 884744 | tf_op jit(solution)/shard_map/ppermute | solution.py:421
  56.0 10.8 %collective-permute-start.12 = (bf16[64,512]{1,0:T(8,128)(2,1)S(1)}, bf16[64,512]{1,0:T(8,128)(2,1)S(1)}, u32[]{:S(2)}, u32[]{:S(2)}) collective-permute-start(bf16[64,512]{1,0:T(8,128)(2,1)S(1)} %get-tuple-element.52), channel_id=1, source_target_pairs={{0,12},{1,13},{2,14},{3,15},{4,0},{5,1},{6,2},{7,3},{8,4},{9,5},{1... | collective-permute-start | bytes 196616 | tf_op jit(solution)/shard_map/ppermute | solution.py:426
  57.0 25.8 %collective-permute-start.13 = (bf16[64,512]{1,0:T(8,128)(2,1)S(1)}, bf16[64,512]{1,0:T(8,128)(2,1)S(1)}, u32[]{:S(2)}, u32[]{:S(2)}) collective-permute-start(bf16[64,512]{1,0:T(8,128)(2,1)S(1)} %get-tuple-element.53), channel_id=1, source_target_pairs={{0,8},{1,9},{2,10},{3,11},{4,12},{5,13},{6,14},{7,15},{8,0},{9,1},... | collective-permute-start | bytes 196616 | tf_op jit(solution)/shard_map/ppermute | solution.py:426
  57.7 25.2 %collective-permute-start.14 = (bf16[64,512]{1,0:T(8,128)(2,1)S(1)}, bf16[64,512]{1,0:T(8,128)(2,1)S(1)}, u32[]{:S(2)}, u32[]{:S(2)}) collective-permute-start(bf16[64,512]{1,0:T(8,128)(2,1)S(1)} %get-tuple-element.54), channel_id=1, source_target_pairs={{0,4},{1,5},{2,6},{3,7},{4,8},{5,9},{6,10},{7,11},{8,12},{9,13},{1... | collective-permute-start | bytes 196616 | tf_op jit(solution)/shard_map/ppermute | solution.py:426
  62.7 20.4 %collective-permute-start.16 = (bf16[64,512]{1,0:T(8,128)(2,1)S(1)}, bf16[64,512]{1,0:T(8,128)(2,1)S(1)}, u32[]{:S(2)}, u32[]{:S(2)}) collective-permute-start(bf16[64,512]{1,0:T(8,128)(2,1)S(1)} %get-tuple-element.60), channel_id=1, source_target_pairs={{0,12},{1,13},{2,14},{3,15},{4,0},{5,1},{6,2},{7,3},{8,4},{9,5},{1... | collective-permute-start | bytes 196616 | tf_op jit(solution)/shard_map/ppermute | solution.py:426
  66.2 16.9 %collective-permute-start.17 = (bf16[64,512]{1,0:T(8,128)(2,1)S(1)}, bf16[64,512]{1,0:T(8,128)(2,1)S(1)}, u32[]{:S(2)}, u32[]{:S(2)}) collective-permute-start(bf16[64,512]{1,0:T(8,128)(2,1)S(1)} %get-tuple-element.61), channel_id=1, source_target_pairs={{0,8},{1,9},{2,10},{3,11},{4,12},{5,13},{6,14},{7,15},{8,0},{9,1},... | collective-permute-start | bytes 196616 | tf_op jit(solution)/shard_map/ppermute | solution.py:426
  66.7 16.4 %collective-permute-start.18 = (bf16[64,512]{1,0:T(8,128)(2,1)S(1)}, bf16[64,512]{1,0:T(8,128)(2,1)S(1)}, u32[]{:S(2)}, u32[]{:S(2)}) collective-permute-start(bf16[64,512]{1,0:T(8,128)(2,1)S(1)} %get-tuple-element.62), channel_id=1, source_target_pairs={{0,4},{1,5},{2,6},{3,7},{4,8},{5,9},{6,10},{7,11},{8,12},{9,13},{1... | collective-permute-start | bytes 196616 | tf_op jit(solution)/shard_map/ppermute | solution.py:426
  82.9 11.6 %copy-start = (bf16[768,768]{1,0:T(8,128)(2,1)S(1)}, bf16[768,768]{1,0:T(8,128)(2,1)}, u32[]{:S(2)}) copy-start(bf16[768,768]{1,0:T(8,128)(2,1)} %refs_4_.1) | copy-start | bytes 3538948
  83.0 2.2 %collective-permute-start.15 = (bf16[4,48,512]{2,1,0:T(8,128)(2,1)S(1)}, bf16[4,48,512]{2,1,0:T(8,128)(2,1)S(1)}, u32[]{:S(2)}, u32[]{:S(2)}) collective-permute-start(bf16[4,48,512]{2,1,0:T(8,128)(2,1)S(1)} %get-tuple-element.56), channel_id=1, source_target_pairs={{0,1},{1,0},{2,3},{3,2},{4,5},{5,4},{6,7},{7,6},{8,9},{9,8},{10,11... | collective-permute-start | bytes 589832 | tf_op jit(solution)/shard_map/ppermute | solution.py:421
  83.3 7.8 %collective-permute-start.19 = (bf16[4,48,512]{2,1,0:T(8,128)(2,1)S(1)}, bf16[4,48,512]{2,1,0:T(8,128)(2,1)S(1)}, u32[]{:S(2)}, u32[]{:S(2)}) collective-permute-start(bf16[4,48,512]{2,1,0:T(8,128)(2,1)S(1)} %get-tuple-element.63), channel_id=1, source_target_pairs={{0,2},{1,3},{2,0},{3,1},{4,6},{5,7},{6,4},{7,5},{8,10},{9,11},{10,... | collective-permute-start | bytes 589832 | tf_op jit(solution)/shard_map/ppermute | solution.py:421
  84.1 10.4 %collective-permute-start.20 = (bf16[4,48,512]{2,1,0:T(8,128)(2,1)S(1)}, bf16[4,48,512]{2,1,0:T(8,128)(2,1)S(1)}, u32[]{:S(2)}, u32[]{:S(2)}) collective-permute-start(bf16[4,48,512]{2,1,0:T(8,128)(2,1)S(1)} %get-tuple-element.64), channel_id=1, source_target_pairs={{0,3},{1,2},{2,1},{3,0},{4,7},{5,6},{6,5},{7,4},{8,11},{9,10},{10,... | collective-permute-start | bytes 589832 | tf_op jit(solution)/shard_map/ppermute | solution.py:421
